TPU v7x, 256 devices: a whole 4x4x8 slice. The times are simulated.
256 devices in a mesh: sub: 64 (over x, z, core), grp: 4 (over y).
Axes of the slice: x: 4, y: 4, z: 8, core: 2. Of those that a mesh axis runs over, the one named last changes fastest.
Arguments:
- block_map: int32 [4, 64, 5], P('grp', 'sub'), may hold values from 0 to 255, as said below
- interior_inverse: bfloat16 [4, 64, 1029, 1029], P('grp', 'sub'), may hold values from -0.1875 to 0.1875
- coupling: bfloat16 [4, 64, 1029, 640], P('grp', 'sub'), may hold values from -1 to 1
- boundary_block: bfloat16 [4, 64, 5, 128, 128], P('grp', 'sub'), may hold values from -6 to 6
- interface_values: float32 [4, 256, 128], P('grp', 'sub'), may hold values from -0.5 to 0.5
- below_weight: float32 [4, 256, 128], P('grp', 'sub'), may hold values from 1 to 8
- above_weight: float32 [4, 256, 128], P('grp', 'sub'), may hold values from 1 to 8
Outputs:
- schur: float32 [4, 64, 5, 128, 128], P('grp', 'sub')
- assembled: float32 [4, 256, 128, 128], P('grp', 'sub')
- product: float32 [4, 256, 128], P('grp', 'sub')
Inputs may be any that keep to these rules, and one draw needn't show every extreme that they name: `block_map`: block g is owned by index g // 4 of sub. The 1 elements of index s of sub name only blocks owned by s or by the indices s + 1, s - 1, s + 2, s - 2, s + 3, s - 3, s + 64 // 2 taken modulo the size of sub; those of any one owner at most 2 times, those of s itself exactly 2 times, those of s + 64 // 2 at least once.
All inputs are finite; a program needn't handle non-finite values.
Results may differ from a plain program's by a relative error of at most 0.0022.
Values sent between devices are 32-bit elements; how exact they have to be, the bound alone decides.
A program may use at most 128 MiB of HBM per device.

v0:
```python
import jax
import jax.numpy as jnp
from jax import lax
from jax.sharding import PartitionSpec as P


def extended(x, sides, width):
    for axis, dim in sides:
        size, length = (lax.axis_size(axis), x.shape[dim])
        up = [(i, (i + 1) % size) for i in range(size - 1)]
        down = [(j, i) for i, j in up]
        last = lax.slice_in_dim(x, length - width, length, axis=dim)
        leading = lax.slice_in_dim(x, 0, width, axis=dim)
        before = lax.ppermute(last, axis, up)
        after = lax.ppermute(leading, axis, down)
        x = jnp.concatenate([before, x, after], axis=dim)
    return x


def shards(
    block_map,
    interior_inverse,
    coupling,
    boundary_block,
    interface_values,
    below_weight,
    above_weight,
):
    inverse = interior_inverse[0, 0]
    coupled = coupling[0]
    elems = coupled.shape[0]
    inner = coupled.shape[1]
    width = interface_values.shape[2]
    owned = interface_values.shape[1]
    nblocks = coupled.shape[2] // width
    solved = jnp.einsum("ij,ejb->eib", inverse, coupled, preferred_element_type=jnp.float32).astype(
        jnp.bfloat16
    )
    cview = coupled.reshape(elems, inner, nblocks, width)
    sview = solved.reshape(elems, inner, nblocks, width)
    correction = jnp.einsum("eika,eikb->ekab", cview, sview, preferred_element_type=jnp.float32)
    diagonal = boundary_block[0].astype(jnp.float32) - correction
    blocks = diagonal.reshape(elems * nblocks, width * width)
    block_ids = block_map[0].reshape(-1)
    rows_here = jnp.arange(owned * lax.axis_size("sub"), dtype=jnp.int32)
    selector = (rows_here[:, None] == block_ids[None, :]).astype(jnp.float32)
    summed = lax.psum_scatter(
        jnp.dot(selector, blocks, precision=lax.Precision.HIGHEST),
        "sub",
        scatter_dimension=0,
        tiled=True,
    )
    assembled = summed.reshape(owned, width, width)
    padded = extended(interface_values, (("grp", 0),), 1)
    applied = jnp.einsum("gab,gb->ga", assembled, padded[1], precision=lax.Precision.HIGHEST)
    product = applied - below_weight[0] * padded[0] - above_weight[0] * padded[2]
    return (diagonal[None], assembled[None], product[None])


def solution(mesh):
    placed = (
        P("grp", "sub", None),
        P("grp", "sub", None, None),
        P("grp", "sub", None, None),
        P("grp", "sub", None, None, None),
        P("grp", "sub", None),
        P("grp", "sub", None),
        P("grp", "sub", None),
    )
    return jax.shard_map(
        shards,
        mesh=mesh,
        in_specs=placed,
        out_specs=(
            P("grp", "sub", None, None, None),
            P("grp", "sub", None, None),
            P("grp", "sub", None),
        ),
        check_vma=False,
    )
```

profile of v0, /device:TPU:1, one launch (start us, length us, event | category | flops | bytes accessed | tf_op | source)
XLA Modules:
  0.0 272.7 jit_solution(17505749763332417758)
XLA Ops:
  7.2 0.0 copy-start
  7.2 0.0 all-reduce.3.cloned.1.call-start
  7.2 3.6 %copy.23 = bf16[1,1,1029,640]{2,3,1,0:T(8,128)(2,1)} copy(bf16[1,1,1029,640]{3,2,1,0:T(8,128)(2,1)} %param.9) | data formatting | bytes 2634240 | tf_op args[2]
  10.9 0.0 copy-done
  10.9 4.6 %fusion = bf16[1,1029,640]{2,1,0:T(8,128)(2,1)} fusion(bf16[1,1,1029,1029]{3,2,1,0:T(8,128)(2,1)S(1)} %copy-done, bf16[1,1,1029,640]{3,2,1,0:T(8,128)(2,1)} %param.9), kind=kOutput, calls=%fused_computation.1 | convolution fusion | flops 1355975040 | bytes 4751922 | tf_op jit(solution)/shard_map/ij,ejb->eib/dot_general | solution.py:36
  15.5 0.0 copy-start.1
  15.5 3.5 %copy.22 = bf16[1,1029,640]{1,2,0:T(8,128)(2,1)} copy(bf16[1,1029,640]{2,1,0:T(8,128)(2,1)} %fusion) | data formatting | bytes 2634240 | tf_op jit(solution)/shard_map/convert_element_type | solution.py:36
  19.0 0.0 copy-done.1
  19.0 0.2 copy.21
  19.2 0.0 copy-start.3
  19.2 2.4 fusion.3
  21.7 0.2 copy.26
  21.8 0.0 copy-done.3
  21.8 9.5 %fusion.4 = f32[256,16384]{1,0:T(8,128)} fusion(f32[1,5,128,128]{3,2,1,0:T(8,128)S(1)} %bitcast.58, s32[5]{0:T(128)S(1)} %bitcast.61), kind=kOutput, calls=%fused_computation.6 | convolution fusion | flops 251659520 | bytes 17104916 | tf_op jit(solution)/shard_map/dot_general | solution.py:48
  31.3 0.0 copy-start.2
  31.3 0.0 copy-start.6
  31.3 0.0 all-reduce.3.cloned.1.call-update
  31.4 0.7 copy-done.2
  32.0 0.0 copy-start.4
  32.0 0.0 copy-start.5
  32.0 4.1 %collective-permute-start = (f32[1,4,128]{2,1,0:T(4,128)S(1)}, f32[1,4,128]{2,1,0:T(4,128)S(1)}, u32[]{:S(2)}, u32[]{:S(2)}) collective-permute-start(f32[1,4,128]{2,1,0:T(4,128)S(1)} %copy-done.2), channel_id=1, source_target_pairs={{0,1},{1,2},{2,3},{4,5},{5,6},{6,7},{8,9},{9,10},{10,11},{12,13},{... | collective-permute-start | bytes 6152 | tf_op jit(solution)/shard_map/ppermute | solution.py:14
  36.2 1.3 collective-permute-start.1
  37.5 0.9 copy.27
  38.4 0.0 copy-done.6
  38.4 0.6 dynamic-slice
  39.6 223.3 %all-reduce.3.cloned.1.call-done = f32[256,16384]{1,0:T(8,128)} async-done(((f32[256,16384]{1,0:T(8,128)}), f32[256,16384]{1,0:T(8,128)}) %all-reduce.3.cloned.1.call-update) | async-done | bytes 16777232
  262.9 1.1 dynamic-slice_bitcast_fusion
  264.0 0.5 fusion.7
  264.5 0.8 copy.44
  265.2 0.0 collective-permute-done
  265.2 0.0 collective-permute-done.1
  265.2 0.0 copy-done.4
  265.2 0.0 copy-done.5
  265.2 0.6 fusion.11
Async XLA Ops:
  7.2 3.7 %copy-start = (bf16[1,1,1029,1029]{3,2,1,0:T(8,128)(2,1)S(1)}, bf16[1,1,1029,1029]{3,2,1,0:T(8,128)(2,1)}, u32[]{:S(2)}) copy-start(bf16[1,1,1029,1029]{3,2,1,0:T(8,128)(2,1)} %param.8) | copy-start | bytes 6353050
  7.2 255.7 %all-reduce.3.cloned.1.call-start = ((), (), s32[]{:S(2)}) async-start(), calls=%async_computation | async-start | bytes 33554432
  15.5 3.5 %copy-start.1 = (bf16[1,1,5,128,128]{4,3,2,1,0:T(8,128)(2,1)S(1)}, bf16[1,1,5,128,128]{4,3,2,1,0:T(8,128)(2,1)}, u32[]{:S(2)}) copy-start(bf16[1,1,5,128,128]{4,3,2,1,0:T(8,128)(2,1)} %param.10) | copy-start | bytes 491524
  19.2 2.6 copy-start.3
  31.3 0.7 copy-start.2
  31.3 7.0 %copy-start.6 = (u32[256]{0:T(256)S(1)}, u32[256]{0:T(256)}, u32[]{:S(2)}) copy-start(u32[256]{0:T(256)} %constant.9) | copy-start | bytes 3076
  32.0 233.2 %copy-start.4 = (f32[1,4,128]{2,1,0:T(4,128)S(1)}, f32[1,4,128]{2,1,0:T(4,128)}, u32[]{:S(2)}) copy-start(f32[1,4,128]{2,1,0:T(4,128)} %param.13) | copy-start | bytes 6148
  32.0 233.2 %copy-start.5 = (f32[1,4,128]{2,1,0:T(4,128)S(1)}, f32[1,4,128]{2,1,0:T(4,128)}, u32[]{:S(2)}) copy-start(f32[1,4,128]{2,1,0:T(4,128)} %param.12) | copy-start | bytes 6148
  32.0 233.2 %collective-permute-start = (f32[1,4,128]{2,1,0:T(4,128)S(1)}, f32[1,4,128]{2,1,0:T(4,128)S(1)}, u32[]{:S(2)}, u32[]{:S(2)}) collective-permute-start(f32[1,4,128]{2,1,0:T(4,128)S(1)} %copy-done.2), channel_id=1, source_target_pairs={{0,1},{1,2},{2,3},{4,5},{5,6},{6,7},{8,9},{9,10},{10,11},{12,13},{... | collective-permute-start | bytes 6152 | tf_op jit(solution)/shard_map/ppermute | solution.py:14
  36.2 229.0 %collective-permute-start.1 = (f32[1,4,128]{2,1,0:T(4,128)S(1)}, f32[1,4,128]{2,1,0:T(4,128)S(1)}, u32[]{:S(2)}, u32[]{:S(2)}) collective-permute-start(f32[1,4,128]{2,1,0:T(4,128)S(1)} %copy-done.2), channel_id=1, source_target_pairs={{1,0},{2,1},{3,2},{5,4},{6,5},{7,6},{9,8},{10,9},{11,10},{13,12},{... | collective-permute-start | bytes 6152 | tf_op jit(solution)/shard_map/ppermute | solution.py:15
Sparse Core Ops, SparseCore 0:
  31.5 231.3 all-reduce.2
where the time goes:
time: 273 us
  waiting for transfers between devices  223 us (82%)
  matrix products  17.1 us (6%)
  between operations  14.8 us (5%)
  local copies, waits for them, and re-layouts  11.5 us (4%)
  starting transfers between devices  5.47 us (2%)
    unnamed x2, waiting for transfers between devices  223 us
    dot_general x1, matrix products, shards(): jnp.dot(selector, blocks, precision=lax.Precision.HIGHEST)  9.49 us
    unnamed x20, local copies, waits for them, and re-layouts  7.81 us
  transfers between devices with their start and end apart: 3, of which 1 were waited for; matrix products, arithmetic and copies ran while one was open for 1% of the time, Pallas kernels for 0%

commit v1 on v0

v1 whole, which is shorter than its diff:
```python
import functools

import jax
import jax.numpy as jnp
from jax import lax
from jax.experimental import pallas as pl
from jax.experimental.pallas import tpu as pltpu
from jax.sharding import PartitionSpec as P

MESH = pl.DeviceIdType.MESH
F32 = jnp.float32
TAG = 8


def arrange(block_map, me, size):
    count = block_map.shape[-1]
    ids = [block_map[0, 0, k] for k in range(count)]
    half = lax.rem(me + size // 2, size)
    keys = []
    seen = jnp.int32(0)
    for block in ids:
        owner = block // 4
        is_half = owner == half
        keys.append(jnp.where(owner == me, 3, jnp.where(is_half, jnp.where(seen > 0, 1, 2), 0)))
        seen = seen + is_half.astype(jnp.int32)
    places = []
    for k in range(count):
        place = jnp.int32(0)
        for j in range(count):
            if j < k:
                place = place + (keys[j] <= keys[k]).astype(jnp.int32)
            elif j > k:
                place = place + (keys[j] < keys[k]).astype(jnp.int32)
        places.append(place)
    order, tags = [], []
    for i in range(count):
        pick, tag = jnp.int32(0), jnp.int32(0)
        for k in range(count):
            pick = pick + jnp.where(places[k] == i, k, 0)
            tag = tag + jnp.where(places[k] == i, ids[k], 0)
        order.append(pick)
        tags.append(tag)
    return places, order, tags


def kernel(
    size,
    groups,
    map_hbm,
    inverse_hbm,
    coupling_hbm,
    boundary_hbm,
    values_hbm,
    below_hbm,
    above_hbm,
    schur_ref,
    assembled_ref,
    product_ref,
    block_map,
    inverse,
    coupling,
    boundary,
    values,
    below,
    above,
    lower,
    upper,
    near,
    cross,
    held,
    inbox,
    load_sem,
    send_sem,
    recv_sem,
):
    me, grp = lax.axis_index("sub"), lax.axis_index("grp")
    core = lax.rem(me, 2)
    flip = 1 - 2 * core
    left, right = lax.rem(me + size - 2, size), lax.rem(me + 2, size)
    twin = me + flip
    far = lax.rem(me + size - 3 * flip, size)
    half = lax.rem(me + size // 2, size)
    down, up = lax.rem(grp + groups - 1, groups), lax.rem(grp + 1, groups)

    loads = [
        pltpu.make_async_copy(source, target, load_sem.at[i])
        for i, (source, target) in enumerate(
            (
                (map_hbm, block_map),
                (inverse_hbm.at[0, 0], inverse),
                (boundary_hbm.at[0, 0], boundary),
                (values_hbm.at[0], values),
                (below_hbm.at[0], below),
                (above_hbm.at[0], above),
                *((coupling_hbm.at[0, 0, :, pl.ds(k * 128, 128)], coupling.at[k]) for k in range(5)),
            )
        )
    ]
    for load in loads:
        load.start()

    barrier = pltpu.get_barrier_semaphore()
    partners = [(left, grp), (right, grp), (twin, grp), (far, grp), (half, grp), (me, down), (me, up)]
    for partner in partners:
        pl.semaphore_signal(barrier, inc=1, device_id=partner, device_id_type=MESH)

    def send(index, source, target, device):
        copy = pltpu.make_async_remote_copy(
            src_ref=source,
            dst_ref=target,
            send_sem=send_sem.at[index],
            recv_sem=recv_sem.at[index],
            device_id=device,
            device_id_type=MESH,
        )
        copy.start()
        return copy

    first, second = pl.ds(0, TAG + 128), pl.ds(TAG + 128, 128)

    loads[0].wait()
    places, order, tags = arrange(block_map, me, size)

    def label(target, numbers):
        rows = lax.broadcasted_iota(jnp.int32, (TAG, 128), 0)
        target[0:TAG, :] = jnp.where(rows == 0, numbers[0], numbers[1]).astype(F32)

    label(near, tags[0:2])
    label(cross, (tags[2], tags[1]))

    for load in loads[6:]:
        load.wait()
    loads[1].wait()
    loads[2].wait()

    def condense(picks):
        blocks = [coupling[pick] for pick in picks]
        wide = jnp.concatenate(blocks, axis=1)
        sums = [None] * len(picks)
        for low, high in ((0, 512), (512, inverse.shape[0])):
            solved = jnp.dot(inverse[low:high, :], wide, preferred_element_type=F32).astype(jnp.bfloat16)
            for i, block in enumerate(blocks):
                part = lax.dot_general(
                    block[low:high],
                    solved[:, i * 128 : (i + 1) * 128],
                    (((0,), (0,)), ((), ())),
                    preferred_element_type=F32,
                )
                sums[i] = part if sums[i] is None else sums[i] + part
        return [boundary[pick].astype(F32) - total for pick, total in zip(picks, sums)]

    ahead = condense(order[0:2])
    near[TAG : TAG + 128, :] = ahead[0]
    near[TAG + 128 : TAG + 256, :] = ahead[1]

    pl.semaphore_wait(barrier, len(partners))
    copies = {}
    for part, rows in enumerate((first, second)):
        copies["left", part] = send(part, near.at[rows], inbox.at[1, rows], (left, grp))
        copies["right", part] = send(2 + part, near.at[rows], inbox.at[0, rows], (right, grp))
        copies["twin", part] = send(4 + part, near.at[rows], inbox.at[2, rows], (twin, grp))
    for part, rows in enumerate((first, second)):
        copies["far", part] = send(6 + part, near.at[rows], inbox.at[3, rows], (far, grp))
    copies["half", 1] = send(8, near.at[second], inbox.at[6, second], (half, grp))
    loads[3].wait()
    copies["up"] = send(9, values, lower, (me, up))
    copies["down"] = send(10, values, upper, (me, down))

    behind = condense(order[2:5])
    cross[TAG : TAG + 128, :] = behind[0]
    copies["half", 0] = send(11, cross, inbox.at[6, first], (half, grp))
    for i, block in enumerate(ahead + behind):
        held[i] = block
    for k in range(5):
        schur_ref[0, 0, k] = held[places[k]]

    owned = assembled_ref.shape[1]
    base = me * owned

    def add(block, tag, start=False):
        for q in range(owned):
            term = jnp.where(tag == base + q, block, 0.0)
            assembled_ref[0, q] = term if start else assembled_ref[0, q] + term

    def add_message(slot, part):
        low = TAG + part * 128
        tag = inbox[slot, part : part + 1, :].astype(jnp.int32)
        add(inbox[slot, low : low + 128, :], tag)

    add(held[3], tags[3], start=True)
    add(held[4], tags[4])

    for part, rows in enumerate((first, second)):
        copies["right", part].wait_recv()
        copies["on_left", part] = send(12 + part, inbox.at[0, rows], inbox.at[4, rows], (twin, grp))
        copies["left", part].wait_recv()
        copies["on_right", part] = send(14 + part, inbox.at[1, rows], inbox.at[5, rows], (twin, grp))
    for part in range(2):
        copies["twin", part].wait_recv()
        add_message(2, part)
    for part in range(2):
        add_message(0, part)
        add_message(1, part)
    for part in range(2):
        copies["half", part].wait_recv()
    for part in range(2):
        add_message(6, part)
    for part in range(2):
        copies["on_left", part].wait_recv()
        add_message(4, part)
        copies["on_right", part].wait_recv()
        add_message(5, part)
    for part in range(2):
        copies["far", part].wait_recv()
        add_message(3, part)

    copies["up"].wait_recv()
    copies["down"].wait_recv()
    loads[4].wait()
    loads[5].wait()
    rows = []
    for q in range(owned):
        terms = assembled_ref[0, q] * values[q : q + 1, :]
        rows.append(jnp.sum(terms.T, axis=0, keepdims=True))
    applied = jnp.concatenate(rows, axis=0)
    under = jnp.where(grp > 0, lower[...], 0.0)
    over = jnp.where(grp < groups - 1, upper[...], 0.0)
    product_ref[0] = applied - below[...] * under - above[...] * over
    for copy in copies.values():
        copy.wait_send()


def shards(block_map, interior_inverse, coupling, boundary_block, interface_values, below_weight, above_weight):
    size, groups = lax.axis_size("sub"), lax.axis_size("grp")
    inner = coupling.shape[2]
    count, width = boundary_block.shape[2:4]
    owned = interface_values.shape[1]
    bf16 = jnp.bfloat16
    pair = TAG + 2 * width
    return pl.pallas_call(
        functools.partial(kernel, size, groups),
        out_shape=(
            jax.ShapeDtypeStruct((1, 1, count, width, width), F32),
            jax.ShapeDtypeStruct((1, owned, width, width), F32),
            jax.ShapeDtypeStruct((1, owned, width), F32),
        ),
        in_specs=[pl.BlockSpec(memory_space=pl.ANY)] * 7,
        out_specs=[pl.BlockSpec(memory_space=pltpu.VMEM)] * 3,
        scratch_shapes=[
            pltpu.SMEM(block_map.shape, jnp.int32),
            pltpu.VMEM((inner, inner), bf16),
            pltpu.VMEM((count, inner, width), bf16),
            pltpu.VMEM((count, width, width), bf16),
            pltpu.VMEM((owned, width), F32),
            pltpu.VMEM((owned, width), F32),
            pltpu.VMEM((owned, width), F32),
            pltpu.VMEM((owned, width), F32),
            pltpu.VMEM((owned, width), F32),
            pltpu.VMEM((pair, width), F32),
            pltpu.VMEM((TAG + width, width), F32),
            pltpu.VMEM((count, width, width), F32),
            pltpu.VMEM((7, pair, width), F32),
            pltpu.SemaphoreType.DMA((11,)),
            pltpu.SemaphoreType.DMA((16,)),
            pltpu.SemaphoreType.DMA((16,)),
        ],
        compiler_params=pltpu.CompilerParams(
            collective_id=0, has_side_effects=True, vmem_limit_bytes=56 * 1024 * 1024
        ),
        name="condense_and_assemble",
    )(block_map, interior_inverse, coupling, boundary_block, interface_values, below_weight, above_weight)


def solution(mesh):
    placed = (
        P("grp", "sub", None),
        P("grp", "sub", None, None),
        P("grp", "sub", None, None),
        P("grp", "sub", None, None, None),
        P("grp", "sub", None),
        P("grp", "sub", None),
        P("grp", "sub", None),
    )
    return jax.shard_map(
        shards,
        mesh=mesh,
        in_specs=placed,
        out_specs=(
            P("grp", "sub", None, None, None),
            P("grp", "sub", None, None),
            P("grp", "sub", None),
        ),
        check_vma=False,
    )
```

time: 273 us -> 25.9 us (0.09)
  waiting for transfers between devices: 223 us -> 0 us
  Pallas kernels: 0 us -> 20.4 us
  matrix products: 17.1 us -> 0 us
  between operations: 14.8 us -> 0.64 us
  local copies, waits for them, and re-layouts: 11.5 us -> 4.64 us
  starting transfers between devices: 5.47 us -> 0 us
    unnamed x2 -> x0, waiting for transfers between devices: 223 us -> none
    pallas_call x0 -> x1, Pallas kernels: none -> 20.4 us  [shards(): pl.pallas_call(functools.partial(kernel, size, groups), out_shape=(jax.Sh...]
    dot_general x4 -> x0, matrix products: 17.1 us -> none  [the longest x1 9.49 us: shards(): jnp.dot(selector, blocks, precision=lax.Precision.HIGHEST)]
    ppermute x2 -> x0, starting transfers between devices: 5.44 us -> none  [the longest x1 4.14 us: extended(): before = lax.ppermute(last, axis, up)]
    convert_element_type x1 -> x0, local copies, waits for them, and re-layouts: 3.52 us -> none  [shards(): jnp.einsum('ij,ejb->eib', inverse, coupled, preferred_element_type=jnp.fl...]
    unnamed x20 -> x3, local copies, waits for them, and re-layouts: 7.81 us -> 4.64 us
  transfers between devices with their start and end apart: 3 -> 0, of which waited for: 1 -> 0; matrix products, arithmetic and copies ran while one was open for 1% -> 0% of each run, Pallas kernels for 0% -> 0%
where the time goes in v1:
time: 25.9 us; the launch traced here: 25.7 us
  Pallas kernels  20.4 us (79%)
  local copies, waits for them, and re-layouts  4.64 us (18%)
  between operations  0.64 us (2%)
    pallas_call x1, Pallas kernels, shards(): pl.pallas_call(functools.partial(kernel, size, groups), out_shape=(jax.Sh...  20.4 us
    unnamed x3, local copies, waits for them, and re-layouts  4.64 us

profile of v1, /device:TPU:1, one launch (start us, length us, event | category | flops | bytes accessed | tf_op | source)
XLA Modules:
  0.0 25.7 jit_solution(15520587789550163416)
XLA Ops:
  0.6 20.4 %condense_and_assemble.1 = (f32[1,1,5,128,128]{4,3,2,1,0:T(8,128)}, f32[1,4,128,128]{3,2,1,0:T(8,128)}, f32[1,4,128]{2,1,0:T(4,128)}) custom-call(s32[1,1,5]{2,1,0:T(1,128)} %map_hbm.1, bf16[1,1,1029,1029]{3,2,1,0:T(8,128)(2,1)} %inverse_hbm.1, bf16[1,1,1029,640]{3,2,1,0:T(8,128)(2,1)} %coupling_hbm.1, bf16[1,1,5,128,128]{4,3,2,1,0:T(8,128)(2,1)} %boundary_hbm.1, ...), custom_call_target="tpu_custom_call" | custom-call | tf_op jit(solution)/shard_map/condense_and_assemble/pallas_call | solution.py:240
  21.0 1.7 %copy.13 = f32[1,1,5,128,128]{4,3,2,1,0:T(8,128)} copy(f32[1,1,5,128,128]{4,3,2,1,0:T(8,128)} %get-tuple-element.6) | data formatting | bytes 655360
  22.8 1.7 %copy.14 = f32[1,4,128,128]{3,2,1,0:T(8,128)} copy(f32[1,4,128,128]{3,2,1,0:T(8,128)} %get-tuple-element.7) | data formatting | bytes 524288
  24.4 1.3 %copy.15 = f32[1,4,128]{2,1,0:T(4,128)} copy(f32[1,4,128]{2,1,0:T(4,128)} %get-tuple-element.8) | data formatting | bytes 4096

commit v2 on v1

--- a/solution.py
+++ b/solution.py
@@ -75,10 +75,10 @@
 ):
     me, grp = lax.axis_index("sub"), lax.axis_index("grp")
     core = lax.rem(me, 2)
-    flip = 1 - 2 * core
-    left, right = lax.rem(me + size - 2, size), lax.rem(me + 2, size)
-    twin = me + flip
-    far = lax.rem(me + size - 3 * flip, size)
+    step = 2 * core - 1
+    twin = lax.rem(me + size - step, size)
+    outer, inner = lax.rem(me + size + 2 * step, size), lax.rem(me + size - 2 * step, size)
+    beyond = lax.rem(me + size + step, size)
     half = lax.rem(me + size // 2, size)
     down, up = lax.rem(grp + groups - 1, groups), lax.rem(grp + 1, groups)
 
@@ -100,7 +100,7 @@
         load.start()
 
     barrier = pltpu.get_barrier_semaphore()
-    partners = [(left, grp), (right, grp), (twin, grp), (far, grp), (half, grp), (me, down), (me, up)]
+    partners = [(outer, grp), (inner, grp), (twin, grp), (beyond, grp), (half, grp), (me, down), (me, up)]
     for partner in partners:
         pl.semaphore_signal(barrier, inc=1, device_id=partner, device_id_type=MESH)
 
@@ -156,11 +156,10 @@
     pl.semaphore_wait(barrier, len(partners))
     copies = {}
     for part, rows in enumerate((first, second)):
-        copies["left", part] = send(part, near.at[rows], inbox.at[1, rows], (left, grp))
-        copies["right", part] = send(2 + part, near.at[rows], inbox.at[0, rows], (right, grp))
+        copies["outer", part] = send(part, near.at[rows], inbox.at[0, rows], (outer, grp))
+        copies["inner", part] = send(2 + part, near.at[rows], inbox.at[1, rows], (inner, grp))
+    for part, rows in enumerate((first, second)):
         copies["twin", part] = send(4 + part, near.at[rows], inbox.at[2, rows], (twin, grp))
-    for part, rows in enumerate((first, second)):
-        copies["far", part] = send(6 + part, near.at[rows], inbox.at[3, rows], (far, grp))
     copies["half", 1] = send(8, near.at[second], inbox.at[6, second], (half, grp))
     loads[3].wait()
     copies["up"] = send(9, values, lower, (me, up))
@@ -172,15 +171,15 @@
     for i, block in enumerate(ahead + behind):
         held[i] = block
     for k in range(5):
-        schur_ref[0, 0, k] = held[places[k]]
-
-    owned = assembled_ref.shape[1]
+        schur_ref[k] = held[places[k]]
+
+    owned = assembled_ref.shape[0]
     base = me * owned
 
     def add(block, tag, start=False):
         for q in range(owned):
             term = jnp.where(tag == base + q, block, 0.0)
-            assembled_ref[0, q] = term if start else assembled_ref[0, q] + term
+            assembled_ref[q] = term if start else assembled_ref[q] + term
 
     def add_message(slot, part):
         low = TAG + part * 128
@@ -191,10 +190,11 @@
     add(held[4], tags[4])
 
     for part, rows in enumerate((first, second)):
-        copies["right", part].wait_recv()
-        copies["on_left", part] = send(12 + part, inbox.at[0, rows], inbox.at[4, rows], (twin, grp))
-        copies["left", part].wait_recv()
-        copies["on_right", part] = send(14 + part, inbox.at[1, rows], inbox.at[5, rows], (twin, grp))
+        copies["outer", part].wait_recv()
+        copies["far", part] = send(6 + part, inbox.at[0, rows], inbox.at[3, rows], (beyond, grp))
+        copies["on_outer", part] = send(12 + part, inbox.at[0, rows], inbox.at[4, rows], (twin, grp))
+        copies["inner", part].wait_recv()
+        copies["on_inner", part] = send(14 + part, inbox.at[1, rows], inbox.at[5, rows], (twin, grp))
     for part in range(2):
         copies["twin", part].wait_recv()
         add_message(2, part)
@@ -206,9 +206,9 @@
     for part in range(2):
         add_message(6, part)
     for part in range(2):
-        copies["on_left", part].wait_recv()
+        copies["on_outer", part].wait_recv()
         add_message(4, part)
-        copies["on_right", part].wait_recv()
+        copies["on_inner", part].wait_recv()
         add_message(5, part)
     for part in range(2):
         copies["far", part].wait_recv()
@@ -220,14 +220,27 @@
     loads[5].wait()
     rows = []
     for q in range(owned):
-        terms = assembled_ref[0, q] * values[q : q + 1, :]
+        terms = assembled_ref[q] * values[q : q + 1, :]
         rows.append(jnp.sum(terms.T, axis=0, keepdims=True))
     applied = jnp.concatenate(rows, axis=0)
     under = jnp.where(grp > 0, lower[...], 0.0)
     over = jnp.where(grp < groups - 1, upper[...], 0.0)
-    product_ref[0] = applied - below[...] * under - above[...] * over
+    product_ref[...] = applied - below[...] * under - above[...] * over
     for copy in copies.values():
         copy.wait_send()
+
+
+def write_out(schur, assembled, product, schur_hbm, assembled_hbm, product_hbm, sem):
+    copies = [
+        pltpu.make_async_copy(source, target, sem.at[i])
+        for i, (source, target) in enumerate(
+            ((schur, schur_hbm.at[0, 0]), (assembled, assembled_hbm.at[0]), (product, product_hbm.at[0]))
+        )
+    ]
+    for copy in copies:
+        copy.start()
+    for copy in copies:
+        copy.wait()
 
 
 def shards(block_map, interior_inverse, coupling, boundary_block, interface_values, below_weight, above_weight):
@@ -237,12 +250,12 @@
     owned = interface_values.shape[1]
     bf16 = jnp.bfloat16
     pair = TAG + 2 * width
-    return pl.pallas_call(
+    results = pl.pallas_call(
         functools.partial(kernel, size, groups),
         out_shape=(
-            jax.ShapeDtypeStruct((1, 1, count, width, width), F32),
-            jax.ShapeDtypeStruct((1, owned, width, width), F32),
-            jax.ShapeDtypeStruct((1, owned, width), F32),
+            pltpu.VMEM((count, width, width), F32),
+            pltpu.VMEM((owned, width, width), F32),
+            pltpu.VMEM((owned, width), F32),
         ),
         in_specs=[pl.BlockSpec(memory_space=pl.ANY)] * 7,
         out_specs=[pl.BlockSpec(memory_space=pltpu.VMEM)] * 3,
@@ -269,6 +282,20 @@
         ),
         name="condense_and_assemble",
     )(block_map, interior_inverse, coupling, boundary_block, interface_values, below_weight, above_weight)
+
+    results = [pltpu.with_memory_space_constraint(x, pltpu.VMEM) for x in results]
+    return pl.pallas_call(
+        write_out,
+        out_shape=(
+            jax.ShapeDtypeStruct((1, 1, count, width, width), F32),
+            jax.ShapeDtypeStruct((1, owned, width, width), F32),
+            jax.ShapeDtypeStruct((1, owned, width), F32),
+        ),
+        in_specs=[pl.BlockSpec(memory_space=pltpu.VMEM)] * 3,
+        out_specs=[pl.BlockSpec(memory_space=pl.ANY)] * 3,
+        scratch_shapes=[pltpu.SemaphoreType.DMA((3,))],
+        name="write_out",
+    )(*results)
 
 
 def solution(mesh):

time: 25.9 us -> 19.9 us (0.77)
  local copies, waits for them, and re-layouts: 4.64 us -> 0 us
  Pallas kernels: 20.4 us -> 19.2 us
    unnamed x3 -> x0, local copies, waits for them, and re-layouts: 4.64 us -> none
    pallas_call x1 -> x2, Pallas kernels: 20.4 us -> 19.2 us  [the longest x1 18.3 us: shards(): pl.pallas_call(functools.partial(kernel, size, groups), out_shape=(pltpu....]
where the time goes in v2:
time: 19.9 us; the launch traced here: 19.8 us
  Pallas kernels  19.2 us (96%)
  between operations  0.64 us (3%)
    pallas_call x1, Pallas kernels, shards(): pl.pallas_call(functools.partial(kernel, size, groups), out_shape=(pltpu....  18.3 us
    pallas_call x1, Pallas kernels, shards(): pl.pallas_call(write_out, out_shape=(jax.ShapeDtypeStruct((1, 1, count, w...  0.84 us

profile of v2, /device:TPU:1, one launch (start us, length us, event | category | flops | bytes accessed | tf_op | source)
XLA Modules:
  0.0 19.8 jit_solution(1889795134690912971)
XLA Ops:
  0.6 18.3 %condense_and_assemble.1 = (f32[5,128,128]{2,1,0:T(8,128)S(1)}, f32[4,128,128]{2,1,0:T(8,128)S(1)}, f32[4,128]{1,0:T(4,128)S(1)}) custom-call(s32[1,1,5]{2,1,0:T(1,128)} %map_hbm.1, bf16[1,1,1029,1029]{3,2,1,0:T(8,128)(2,1)} %inverse_hbm.1, bf16[1,1,1029,640]{3,2,1,0:T(8,128)(2,1)} %coupling_hbm.1, bf16[1,1,5,128,128]{4,3,2,1,0:T(8,128)(2,1)} %boundary_hbm.1, ...), custom_call_target="tpu_custom_call" | custom-call | tf_op jit(solution)/shard_map/condense_and_assemble/pallas_call | solution.py:253
  19.0 0.8 %write_out.1 = (f32[1,1,5,128,128]{4,3,2,1,0:T(8,128)}, f32[1,4,128,128]{3,2,1,0:T(8,128)}, f32[1,4,128]{2,1,0:T(4,128)}) custom-call(f32[5,128,128]{2,1,0:T(8,128)S(1)} %get-tuple-element.6.schur, f32[4,128,128]{2,1,0:T(8,128)S(1)} %get-tuple-element.7.assembled, f32[4,128]{1,0:T(4,128)S(1)} %get-tuple-element.8.product), custom_call_target="tpu_custom_call" | custom-call | tf_op jit(solution)/shard_map/write_out/pallas_call | solution.py:287

commit v3 on v2

--- a/solution.py
+++ b/solution.py
@@ -9,6 +9,7 @@
 
 MESH = pl.DeviceIdType.MESH
 F32 = jnp.float32
+PLANES = 8
 TAG = 8
 
 
@@ -72,14 +73,22 @@
     load_sem,
     send_sem,
     recv_sem,
+    ready,
 ):
     me, grp = lax.axis_index("sub"), lax.axis_index("grp")
     core = lax.rem(me, 2)
     step = 2 * core - 1
     twin = lax.rem(me + size - step, size)
-    outer, inner = lax.rem(me + size + 2 * step, size), lax.rem(me + size - 2 * step, size)
+    outer = lax.rem(me + size + 2 * step, size)
+    behind = lax.rem(me + size - 2 * step, size)
+    inner = lax.rem(me + size - 3 * step, size)
     beyond = lax.rem(me + size + step, size)
     half = lax.rem(me + size // 2, size)
+    plane = lax.rem(me // 2, PLANES)
+    bottom, top = plane == 0, plane == PLANES - 1
+    odd = core == 1
+    bottom_odd, bottom_even = jnp.logical_and(bottom, odd), jnp.logical_and(bottom, core == 0)
+    top_odd, top_even = jnp.logical_and(top, odd), jnp.logical_and(top, core == 0)
     down, up = lax.rem(grp + groups - 1, groups), lax.rem(grp + 1, groups)
 
     loads = [
@@ -100,12 +109,22 @@
         load.start()
 
     barrier = pltpu.get_barrier_semaphore()
-    partners = [(outer, grp), (inner, grp), (twin, grp), (beyond, grp), (half, grp), (me, down), (me, up)]
-    for partner in partners:
-        pl.semaphore_signal(barrier, inc=1, device_id=partner, device_id_type=MESH)
-
-    def send(index, source, target, device):
-        copy = pltpu.make_async_remote_copy(
+    def signal(semaphore, *peers):
+        for peer in peers:
+            pl.semaphore_signal(semaphore, inc=1, device_id=peer, device_id_type=MESH)
+
+    signal(barrier, (twin, grp), (half, grp), (me, down), (me, up))
+
+    @pl.when(jnp.logical_not(top_odd))
+    def _():
+        signal(barrier, (outer, grp), (beyond, grp))
+
+    @pl.when(jnp.logical_not(top_even))
+    def _():
+        signal(barrier, (behind, grp), (inner, grp))
+
+    def describe(index, source, target, device):
+        return pltpu.make_async_remote_copy(
             src_ref=source,
             dst_ref=target,
             send_sem=send_sem.at[index],
@@ -113,6 +132,9 @@
             device_id=device,
             device_id_type=MESH,
         )
+
+    def send(*args):
+        copy = describe(*args)
         copy.start()
         return copy
 
@@ -153,11 +175,22 @@
     near[TAG : TAG + 128, :] = ahead[0]
     near[TAG + 128 : TAG + 256, :] = ahead[1]
 
-    pl.semaphore_wait(barrier, len(partners))
+    pl.semaphore_wait(barrier, 8 - 2 * bottom.astype(jnp.int32))
+
+    @pl.when(top_odd)
+    def _():
+        signal(ready, (outer, grp), (beyond, grp))
+
+    @pl.when(top_even)
+    def _():
+        signal(ready, (behind, grp), (inner, grp))
+
     copies = {}
     for part, rows in enumerate((first, second)):
-        copies["outer", part] = send(part, near.at[rows], inbox.at[0, rows], (outer, grp))
-        copies["inner", part] = send(2 + part, near.at[rows], inbox.at[1, rows], (inner, grp))
+        copies["outer", part] = describe(part, near.at[rows], inbox.at[0, rows], (outer, grp))
+        copies["inner", part] = describe(2 + part, near.at[rows], inbox.at[1, rows], (inner, grp))
+        pl.when(jnp.logical_not(bottom_even))(copies["outer", part].start)
+        pl.when(jnp.logical_not(bottom_odd))(copies["inner", part].start)
     for part, rows in enumerate((first, second)):
         copies["twin", part] = send(4 + part, near.at[rows], inbox.at[2, rows], (twin, grp))
     copies["half", 1] = send(8, near.at[second], inbox.at[6, second], (half, grp))
@@ -165,10 +198,18 @@
     copies["up"] = send(9, values, lower, (me, up))
     copies["down"] = send(10, values, upper, (me, down))
 
-    behind = condense(order[2:5])
-    cross[TAG : TAG + 128, :] = behind[0]
+    later = condense(order[2:5])
+    cross[TAG : TAG + 128, :] = later[0]
     copies["half", 0] = send(11, cross, inbox.at[6, first], (half, grp))
-    for i, block in enumerate(ahead + behind):
+
+    @pl.when(bottom)
+    def _():
+        pl.semaphore_wait(ready, 2)
+
+    for part in range(2):
+        pl.when(bottom_even)(copies["outer", part].start)
+        pl.when(bottom_odd)(copies["inner", part].start)
+    for i, block in enumerate(ahead + later):
         held[i] = block
     for k in range(5):
         schur_ref[k] = held[places[k]]
@@ -276,6 +317,7 @@
             pltpu.SemaphoreType.DMA((11,)),
             pltpu.SemaphoreType.DMA((16,)),
             pltpu.SemaphoreType.DMA((16,)),
+            pltpu.SemaphoreType.REGULAR,
         ],
         compiler_params=pltpu.CompilerParams(
             collective_id=0, has_side_effects=True, vmem_limit_bytes=56 * 1024 * 1024

time: 19.9 us -> 19.3 us (0.970)
  Pallas kernels: 19.2 us -> 18.6 us
    pallas_call x1, Pallas kernels: 18.3 us -> 17.8 us  [shards(): pl.pallas_call(functools.partial(kernel, size, groups), out_shape=(pltpu....]
where the time goes in v3:
time: 19.3 us; the launch traced here: 19.2 us
  Pallas kernels  18.6 us (96%)
  between operations  0.64 us (3%)
    pallas_call x1, Pallas kernels, shards(): pl.pallas_call(functools.partial(kernel, size, groups), out_shape=(pltpu....  17.8 us
    pallas_call x1, Pallas kernels, shards(): pl.pallas_call(write_out, out_shape=(jax.ShapeDtypeStruct((1, 1, count, w...  0.84 us

profile of v3, /device:TPU:1, one launch (start us, length us, event | category | flops | bytes accessed | tf_op | source)
XLA Modules:
  0.0 19.2 jit_solution(14794457886953174207)
XLA Ops:
  0.6 17.8 %condense_and_assemble.1 = (f32[5,128,128]{2,1,0:T(8,128)S(1)}, f32[4,128,128]{2,1,0:T(8,128)S(1)}, f32[4,128]{1,0:T(4,128)S(1)}) custom-call(s32[1,1,5]{2,1,0:T(1,128)} %map_hbm.1, bf16[1,1,1029,1029]{3,2,1,0:T(8,128)(2,1)} %inverse_hbm.1, bf16[1,1,1029,640]{3,2,1,0:T(8,128)(2,1)} %coupling_hbm.1, bf16[1,1,5,128,128]{4,3,2,1,0:T(8,128)(2,1)} %boundary_hbm.1, ...), custom_call_target="tpu_custom_call" | custom-call | tf_op jit(solution)/shard_map/condense_and_assemble/pallas_call | solution.py:294
  18.4 0.8 %write_out.1 = (f32[1,1,5,128,128]{4,3,2,1,0:T(8,128)}, f32[1,4,128,128]{3,2,1,0:T(8,128)}, f32[1,4,128]{2,1,0:T(4,128)}) custom-call(f32[5,128,128]{2,1,0:T(8,128)S(1)} %get-tuple-element.6.schur, f32[4,128,128]{2,1,0:T(8,128)S(1)} %get-tuple-element.7.assembled, f32[4,128]{1,0:T(4,128)S(1)} %get-tuple-element.8.product), custom_call_target="tpu_custom_call" | custom-call | tf_op jit(solution)/shard_map/write_out/pallas_call | solution.py:329

commit v4 on v3

--- a/solution.py
+++ b/solution.py
@@ -177,20 +177,21 @@
 
     pl.semaphore_wait(barrier, 8 - 2 * bottom.astype(jnp.int32))
 
-    @pl.when(top_odd)
-    def _():
-        signal(ready, (outer, grp), (beyond, grp))
-
-    @pl.when(top_even)
-    def _():
-        signal(ready, (behind, grp), (inner, grp))
-
     copies = {}
     for part, rows in enumerate((first, second)):
         copies["outer", part] = describe(part, near.at[rows], inbox.at[0, rows], (outer, grp))
         copies["inner", part] = describe(2 + part, near.at[rows], inbox.at[1, rows], (inner, grp))
         pl.when(jnp.logical_not(bottom_even))(copies["outer", part].start)
-        pl.when(jnp.logical_not(bottom_odd))(copies["inner", part].start)
+        pl.when(top)(copies["inner", part].start)
+
+    @pl.when(top_odd)
+    def _():
+        signal(ready, (outer, grp), (beyond, grp))
+
+    @pl.when(top_even)
+    def _():
+        signal(ready, (behind, grp), (inner, grp))
+
     for part, rows in enumerate((first, second)):
         copies["twin", part] = send(4 + part, near.at[rows], inbox.at[2, rows], (twin, grp))
     copies["half", 1] = send(8, near.at[second], inbox.at[6, second], (half, grp))
@@ -198,9 +199,12 @@
     copies["up"] = send(9, values, lower, (me, up))
     copies["down"] = send(10, values, upper, (me, down))
 
-    later = condense(order[2:5])
+    later = condense(order[2:3])
     cross[TAG : TAG + 128, :] = later[0]
     copies["half", 0] = send(11, cross, inbox.at[6, first], (half, grp))
+    for part in range(2):
+        pl.when(jnp.logical_not(jnp.logical_or(top, bottom_odd)))(copies["inner", part].start)
+    later += condense(order[3:5])
 
     @pl.when(bottom)
     def _():
@@ -230,15 +234,16 @@
     add(held[3], tags[3], start=True)
     add(held[4], tags[4])
 
+    for part in range(2):
+        copies["twin", part].wait_recv()
+        add_message(2, part)
     for part, rows in enumerate((first, second)):
         copies["outer", part].wait_recv()
+        copies["on_outer", part] = send(12 + part, inbox.at[0, rows], inbox.at[4, rows], (twin, grp))
         copies["far", part] = send(6 + part, inbox.at[0, rows], inbox.at[3, rows], (beyond, grp))
-        copies["on_outer", part] = send(12 + part, inbox.at[0, rows], inbox.at[4, rows], (twin, grp))
+    for part, rows in enumerate((first, second)):
         copies["inner", part].wait_recv()
         copies["on_inner", part] = send(14 + part, inbox.at[1, rows], inbox.at[5, rows], (twin, grp))
-    for part in range(2):
-        copies["twin", part].wait_recv()
-        add_message(2, part)
     for part in range(2):
         add_message(0, part)
         add_message(1, part)

time: 19.3 us -> 19.2 us (level)
  no operation moved by 1% of the time
where the time goes in v4:
time: 19.2 us; the launch traced here: 19.1 us
  Pallas kernels  18.5 us (96%)
  between operations  0.64 us (3%)
    pallas_call x1, Pallas kernels, shards(): pl.pallas_call(functools.partial(kernel, size, groups), out_shape=(pltpu....  17.6 us
    pallas_call x1, Pallas kernels, shards(): pl.pallas_call(write_out, out_shape=(jax.ShapeDtypeStruct((1, 1, count, w...  0.84 us

profile of v4, /device:TPU:1, one launch (start us, length us, event | category | flops | bytes accessed | tf_op | source)
XLA Modules:
  0.0 19.1 jit_solution(4500383206129026437)
XLA Ops:
  0.6 17.6 %condense_and_assemble.1 = (f32[5,128,128]{2,1,0:T(8,128)S(1)}, f32[4,128,128]{2,1,0:T(8,128)S(1)}, f32[4,128]{1,0:T(4,128)S(1)}) custom-call(s32[1,1,5]{2,1,0:T(1,128)} %map_hbm.1, bf16[1,1,1029,1029]{3,2,1,0:T(8,128)(2,1)} %inverse_hbm.1, bf16[1,1,1029,640]{3,2,1,0:T(8,128)(2,1)} %coupling_hbm.1, bf16[1,1,5,128,128]{4,3,2,1,0:T(8,128)(2,1)} %boundary_hbm.1, ...), custom_call_target="tpu_custom_call" | custom-call | tf_op jit(solution)/shard_map/condense_and_assemble/pallas_call | solution.py:299
  18.3 0.8 %write_out.1 = (f32[1,1,5,128,128]{4,3,2,1,0:T(8,128)}, f32[1,4,128,128]{3,2,1,0:T(8,128)}, f32[1,4,128]{2,1,0:T(4,128)}) custom-call(f32[5,128,128]{2,1,0:T(8,128)S(1)} %get-tuple-element.6.schur, f32[4,128,128]{2,1,0:T(8,128)S(1)} %get-tuple-element.7.assembled, f32[4,128]{1,0:T(4,128)S(1)} %get-tuple-element.8.product), custom_call_target="tpu_custom_call" | custom-call | tf_op jit(solution)/shard_map/write_out/pallas_call | solution.py:334

commit v5 on v4

--- a/solution.py
+++ b/solution.py
@@ -192,18 +192,18 @@
     def _():
         signal(ready, (behind, grp), (inner, grp))
 
+    copies["half", 1] = send(8, near.at[second], inbox.at[6, second], (half, grp))
+
+    later = condense(order[2:3])
+    cross[TAG : TAG + 128, :] = later[0]
+    copies["half", 0] = send(11, cross, inbox.at[6, first], (half, grp))
+    for part in range(2):
+        pl.when(jnp.logical_not(jnp.logical_or(top, bottom_odd)))(copies["inner", part].start)
     for part, rows in enumerate((first, second)):
         copies["twin", part] = send(4 + part, near.at[rows], inbox.at[2, rows], (twin, grp))
-    copies["half", 1] = send(8, near.at[second], inbox.at[6, second], (half, grp))
     loads[3].wait()
     copies["up"] = send(9, values, lower, (me, up))
     copies["down"] = send(10, values, upper, (me, down))
-
-    later = condense(order[2:3])
-    cross[TAG : TAG + 128, :] = later[0]
-    copies["half", 0] = send(11, cross, inbox.at[6, first], (half, grp))
-    for part in range(2):
-        pl.when(jnp.logical_not(jnp.logical_or(top, bottom_odd)))(copies["inner", part].start)
     later += condense(order[3:5])
 
     @pl.when(bottom)

time: 19.2 us -> 19 us (0.990)
  Pallas kernels: 18.5 us -> 18.2 us
    pallas_call x1, Pallas kernels: 17.6 us -> 17.4 us  [shards(): pl.pallas_call(functools.partial(kernel, size, groups), out_shape=(pltpu....]
where the time goes in v5:
time: 19 us; the launch traced here: 18.9 us
  Pallas kernels  18.2 us (96%)
  between operations  0.64 us (3%)
    pallas_call x1, Pallas kernels, shards(): pl.pallas_call(functools.partial(kernel, size, groups), out_shape=(pltpu....  17.4 us
    pallas_call x1, Pallas kernels, shards(): pl.pallas_call(write_out, out_shape=(jax.ShapeDtypeStruct((1, 1, count, w...  0.84 us

profile of v5, /device:TPU:1, one launch (start us, length us, event | category | flops | bytes accessed | tf_op | source)
XLA Modules:
  0.0 18.9 jit_solution(6436286479790433278)
XLA Ops:
  0.6 17.4 %condense_and_assemble.1 = (f32[5,128,128]{2,1,0:T(8,128)S(1)}, f32[4,128,128]{2,1,0:T(8,128)S(1)}, f32[4,128]{1,0:T(4,128)S(1)}) custom-call(s32[1,1,5]{2,1,0:T(1,128)} %map_hbm.1, bf16[1,1,1029,1029]{3,2,1,0:T(8,128)(2,1)} %inverse_hbm.1, bf16[1,1,1029,640]{3,2,1,0:T(8,128)(2,1)} %coupling_hbm.1, bf16[1,1,5,128,128]{4,3,2,1,0:T(8,128)(2,1)} %boundary_hbm.1, ...), custom_call_target="tpu_custom_call" | custom-call | tf_op jit(solution)/shard_map/condense_and_assemble/pallas_call | solution.py:299
  18.0 0.8 %write_out.1 = (f32[1,1,5,128,128]{4,3,2,1,0:T(8,128)}, f32[1,4,128,128]{3,2,1,0:T(8,128)}, f32[1,4,128]{2,1,0:T(4,128)}) custom-call(f32[5,128,128]{2,1,0:T(8,128)S(1)} %get-tuple-element.6.schur, f32[4,128,128]{2,1,0:T(8,128)S(1)} %get-tuple-element.7.assembled, f32[4,128]{1,0:T(4,128)S(1)} %get-tuple-element.8.product), custom_call_target="tpu_custom_call" | custom-call | tf_op jit(solution)/shard_map/write_out/pallas_call | solution.py:334

commit v6 on v5

--- a/solution.py
+++ b/solution.py
@@ -192,11 +192,11 @@
     def _():
         signal(ready, (behind, grp), (inner, grp))
 
-    copies["half", 1] = send(8, near.at[second], inbox.at[6, second], (half, grp))
 
     later = condense(order[2:3])
     cross[TAG : TAG + 128, :] = later[0]
     copies["half", 0] = send(11, cross, inbox.at[6, first], (half, grp))
+    copies["half", 1] = send(8, near.at[second], inbox.at[6, second], (half, grp))
     for part in range(2):
         pl.when(jnp.logical_not(jnp.logical_or(top, bottom_odd)))(copies["inner", part].start)
     for part, rows in enumerate((first, second)):

time: 19 us -> 19 us (level)
  no operation moved by 1% of the time
where the time goes in v6:
time: 19 us; the launch traced here: 18.9 us
  Pallas kernels  18.2 us (96%)
  between operations  0.64 us (3%)
    pallas_call x1, Pallas kernels, shards(): pl.pallas_call(functools.partial(kernel, size, groups), out_shape=(pltpu....  17.4 us
    pallas_call x1, Pallas kernels, shards(): pl.pallas_call(write_out, out_shape=(jax.ShapeDtypeStruct((1, 1, count, w...  0.84 us

profile of v6, /device:TPU:1, one launch (start us, length us, event | category | flops | bytes accessed | tf_op | source)
XLA Modules:
  0.0 18.9 jit_solution(6804129104623962254)
XLA Ops:
  0.6 17.4 %condense_and_assemble.1 = (f32[5,128,128]{2,1,0:T(8,128)S(1)}, f32[4,128,128]{2,1,0:T(8,128)S(1)}, f32[4,128]{1,0:T(4,128)S(1)}) custom-call(s32[1,1,5]{2,1,0:T(1,128)} %map_hbm.1, bf16[1,1,1029,1029]{3,2,1,0:T(8,128)(2,1)} %inverse_hbm.1, bf16[1,1,1029,640]{3,2,1,0:T(8,128)(2,1)} %coupling_hbm.1, bf16[1,1,5,128,128]{4,3,2,1,0:T(8,128)(2,1)} %boundary_hbm.1, ...), custom_call_target="tpu_custom_call" | custom-call | tf_op jit(solution)/shard_map/condense_and_assemble/pallas_call | solution.py:299
  18.0 0.8 %write_out.1 = (f32[1,1,5,128,128]{4,3,2,1,0:T(8,128)}, f32[1,4,128,128]{3,2,1,0:T(8,128)}, f32[1,4,128]{2,1,0:T(4,128)}) custom-call(f32[5,128,128]{2,1,0:T(8,128)S(1)} %get-tuple-element.6.schur, f32[4,128,128]{2,1,0:T(8,128)S(1)} %get-tuple-element.7.assembled, f32[4,128]{1,0:T(4,128)S(1)} %get-tuple-element.8.product), custom_call_target="tpu_custom_call" | custom-call | tf_op jit(solution)/shard_map/write_out/pallas_call | solution.py:334

commit v7 on v5

--- a/solution.py
+++ b/solution.py
@@ -105,7 +105,7 @@
             )
         )
     ]
-    for load in loads:
+    for load in loads[:2] + loads[6:] + loads[2:6]:
         load.start()
 
     barrier = pltpu.get_barrier_semaphore()

time: 19 us -> 18.9 us (level)
  no operation moved by 1% of the time
where the time goes in v7:
time: 18.9 us; the launch traced here: 18.8 us
  Pallas kernels  18.2 us (96%)
  between operations  0.64 us (3%)
    pallas_call x1, Pallas kernels, shards(): pl.pallas_call(functools.partial(kernel, size, groups), out_shape=(pltpu....  17.4 us
    pallas_call x1, Pallas kernels, shards(): pl.pallas_call(write_out, out_shape=(jax.ShapeDtypeStruct((1, 1, count, w...  0.84 us

profile of v7, /device:TPU:1, one launch (start us, length us, event | category | flops | bytes accessed | tf_op | source)
XLA Modules:
  0.0 18.8 jit_solution(6149001302395212272)
XLA Ops:
  0.6 17.4 %condense_and_assemble.1 = (f32[5,128,128]{2,1,0:T(8,128)S(1)}, f32[4,128,128]{2,1,0:T(8,128)S(1)}, f32[4,128]{1,0:T(4,128)S(1)}) custom-call(s32[1,1,5]{2,1,0:T(1,128)} %map_hbm.1, bf16[1,1,1029,1029]{3,2,1,0:T(8,128)(2,1)} %inverse_hbm.1, bf16[1,1,1029,640]{3,2,1,0:T(8,128)(2,1)} %coupling_hbm.1, bf16[1,1,5,128,128]{4,3,2,1,0:T(8,128)(2,1)} %boundary_hbm.1, ...), custom_call_target="tpu_custom_call" | custom-call | tf_op jit(solution)/shard_map/condense_and_assemble/pallas_call | solution.py:299
  18.0 0.8 %write_out.1 = (f32[1,1,5,128,128]{4,3,2,1,0:T(8,128)}, f32[1,4,128,128]{3,2,1,0:T(8,128)}, f32[1,4,128]{2,1,0:T(4,128)}) custom-call(f32[5,128,128]{2,1,0:T(8,128)S(1)} %get-tuple-element.6.schur, f32[4,128,128]{2,1,0:T(8,128)S(1)} %get-tuple-element.7.assembled, f32[4,128]{1,0:T(4,128)S(1)} %get-tuple-element.8.product), custom_call_target="tpu_custom_call" | custom-call | tf_op jit(solution)/shard_map/write_out/pallas_call | solution.py:334
